TPU v7x, 256 devices: a whole 4x4x8 slice. The times are simulated.
256 devices in a mesh: dp: 64 (over z, y, core), fsdp: 4 (over x).
Axes of the slice: x: 4, y: 4, z: 8, core: 2. Of those that a mesh axis runs over, the one named last changes fastest.
Arguments:
- hidden: bfloat16 [65536, 14336], P(('dp', 'fsdp')), may hold values from -6 to 6
- out_grads: bfloat16 [65536, 8192], P(('dp', 'fsdp')), may hold values from -150 to 150
- in_proj: bfloat16 [64, 14336], P(None, 'fsdp'), may hold values from -0.046875 to 0.046875
- out_proj: bfloat16 [64, 8192], P(None, 'fsdp'), may hold values from -0.0625 to 0.0625
- queries: bfloat16 [256, 4096], P(('dp', 'fsdp')), may hold values from -6 to 6
Outputs:
- scores: float32 [256, 512], P(None, ('dp', 'fsdp'))
All inputs are finite; a program needn't handle non-finite values.
Results may differ from a plain program's by a relative error of at most 0.013.
Values may be sent and summed in bfloat16 or wider, within the bound.
A program may use at most 128 MiB of HBM per device.

v0:
```python
import jax
import jax.numpy as jnp
from jax import lax
from jax.sharding import PartitionSpec as P

LEN = 128


def project(rows, matrix):
    return lax.dot_general(
        rows, matrix, (((1,), (1,)), ((), ())), preferred_element_type=jnp.float32
    )


def shards(hidden, out_grads, in_proj, out_proj, queries):
    row_count = hidden.shape[0]
    sketch_rank = in_proj.shape[0]
    seq_count = row_count // LEN
    columns = hidden
    in_side = project(columns, lax.all_gather(in_proj, "fsdp", axis=1, tiled=True))
    columns = out_grads
    out_side = project(columns, lax.all_gather(out_proj, "fsdp", axis=1, tiled=True))
    in_blocks = in_side.reshape(seq_count, LEN, sketch_rank)
    out_blocks = out_side.reshape(seq_count, LEN, sketch_rank)
    outer = jnp.einsum("slb,sla->sba", out_blocks, in_blocks) / jnp.sqrt(jnp.float32(LEN))
    own_sketch = outer.reshape(seq_count, sketch_rank * sketch_rank).astype(jnp.bfloat16)
    all_queries = lax.all_gather(queries, ("dp", "fsdp"), axis=0, tiled=True)
    all_sketch = lax.all_gather(own_sketch, ("dp", "fsdp"), axis=0, tiled=True)
    gram = project(all_sketch, all_sketch)
    cross = project(all_sketch, all_queries)
    examples = gram.shape[0]
    wide = own_sketch.astype(jnp.float32)
    trace_value = lax.psum(jnp.sum(wide * wide), ("dp", "fsdp"))
    damping = 0.1 * trace_value / examples
    system = gram + damping * jnp.eye(examples, dtype=jnp.float32)
    factor = jnp.linalg.cholesky(system)
    middle = lax.linalg.triangular_solve(factor, cross, left_side=True, lower=True)
    solved = lax.linalg.triangular_solve(
        factor, middle, left_side=True, lower=True, transpose_a=True
    )
    first = lax.axis_index(("dp", "fsdp")) * seq_count
    own_rows = lax.dynamic_slice_in_dim(solved, first, seq_count, 0)
    return damping / sketch_rank * own_rows.T


def solution(mesh):
    in_specs = (
        P(("dp", "fsdp"), None),
        P(("dp", "fsdp"), None),
        P(None, "fsdp"),
        P(None, "fsdp"),
        P(("dp", "fsdp"), None),
    )
    out_specs = P(None, ("dp", "fsdp"))
    return jax.shard_map(shards, mesh=mesh, in_specs=in_specs, out_specs=out_specs, check_vma=False)
```

profile of v0, /device:TPU:1, one launch (start us, length us, event | category | flops | bytes accessed | tf_op | source)
XLA Modules:
  0.0 358.7 jit_solution(13208346266131600879)
XLA Ops:
  6.5 0.7 all-gather.7.cloned.1.call-update
  8.1 30.5 %all-gather.7.cloned.1.call-done = bf16[64,8192]{1,0:T(8,128)(2,1)} async-done(((bf16[64,2048]{1,0:T(8,128)(2,1)}), bf16[64,8192]{1,0:T(8,128)(2,1)}) %all-gather.7.cloned.1.call-update) | async-done | bytes 1048592 | tf_op jit(solution)/shard_map/all_gather | solution.py:22
  38.6 3.9 %convolution_bitcast_fusion.1 = bf16[8,2,8,128]{3,2,1,0:T(8,128)(2,1)S(1)} fusion(bf16[256,8192]{1,0:T(8,128)(2,1)} %param.6, bf16[64,8192]{1,0:T(8,128)(2,1)} %all-gather.7.cloned.1.call-done), kind=kOutput, calls=%fused_computation.18 | convolution fusion | flops 268435456 | bytes 5275648 | tf_op jit(solution)/shard_map/dot_general | solution.py:10
  42.5 30.4 %all-gather.9.cloned.1.call-done = bf16[64,14336]{1,0:T(8,128)(2,1)} async-done(((bf16[64,3584]{1,0:T(8,128)(2,1)}), bf16[64,14336]{1,0:T(8,128)(2,1)}) %all-gather.9.cloned.1.call-update) | async-done | bytes 1835024 | tf_op jit(solution)/shard_map/all_gather | solution.py:20
  72.9 6.0 %convolution_bitcast_fusion = bf16[8,2,8,128]{3,2,1,0:T(8,128)(2,1)S(1)} fusion(bf16[256,14336]{1,0:T(8,128)(2,1)} %param.5, bf16[64,14336]{1,0:T(8,128)(2,1)} %all-gather.9.cloned.1.call-done), kind=kOutput, calls=%fused_computation.17 | convolution fusion | flops 469762048 | bytes 9207808 | tf_op jit(solution)/shard_map/dot_general | solution.py:10
  78.9 0.8 multiply_reduce_fusion
  81.0 76.6 %psum.7 = f32[]{:T(128)} all-reduce(f32[]{:T(128)} %get-tuple-element.33), channel_id=1, replica_groups=mesh['dp'=64,'fsdp'=4] {'dp','fsdp'}, use_global_device_ids=true, to_apply=%region_1.0 | all-reduce | flops 1 | bytes 8 | tf_op jit(solution)/shard_map/psum | solution.py:33
  159.0 37.1 %all-gather.11.cloned.1.call-done = bf16[256,2,4096]{2,1,0:T(2,128)(2,1)} async-done(((bf16[1,2,4096]{2,1,0:T(2,128)(2,1)}), bf16[256,2,4096]{2,1,0:T(2,128)(2,1)}) %all-gather.11.cloned.1.call-update) | async-done | bytes 4194320 | tf_op jit(solution)/shard_map/all_gather | solution.py:28
  196.1 7.6 %reshape.73 = bf16[512,4096]{1,0:T(8,128)(2,1)} reshape(bf16[256,2,4096]{2,1,0:T(2,128)(2,1)} %all-gather.11.cloned.1.call-done) | data formatting | bytes 8388608
  203.8 5.8 %fusion.60 = f32[512,512]{1,0:T(8,128)S(1)} fusion(bf16[512,4096]{1,0:T(8,128)(2,1)} %reshape.73), kind=kOutput, calls=%fused_computation.109 | convolution fusion | flops 2147483648 | bytes 5242880 | tf_op jit(solution)/shard_map/dot_general | solution.py:10
  210.2 11.7 %cholesky.103 = f32[128,128]{1,0:T(8,128)S(1)} custom-call(f32[128,128]{1,0:T(8,128)S(1)} %cholesky.263), custom_call_target="Cholesky" | custom-call | tf_op jit(solution)/shard_map/jit(cholesky)/cholesky | solution.py:36
  222.1 9.8 %custom-call.32 = f32[1,128,128]{1,2,0:T(8,128)S(1)} custom-call(f32[1,128,128]{2,1,0:T(8,128)S(1)} %get-tuple-element.32), custom_call_target="InvertDiagBlocksLowerTriangular" | custom-call | tf_op jit(solution)/shard_map/jit(cholesky)/cholesky | solution.py:36
  232.6 11.9 %cholesky.215 = f32[128,128]{1,0:T(8,128)S(1)} custom-call(f32[128,128]{1,0:T(8,128)S(1)} %cholesky.267), custom_call_target="Cholesky" | custom-call | tf_op jit(solution)/shard_map/jit(cholesky)/cholesky | solution.py:36
  244.5 9.8 %custom-call.33 = f32[1,128,128]{1,2,0:T(8,128)S(1)} custom-call(f32[1,128,128]{2,1,0:T(8,128)S(1)} %get-tuple-element.29), custom_call_target="InvertDiagBlocksLowerTriangular" | custom-call | tf_op jit(solution)/shard_map/jit(cholesky)/cholesky | solution.py:36
  255.0 11.7 %cholesky.236 = f32[128,128]{1,0:T(8,128)S(1)} custom-call(f32[128,128]{1,0:T(8,128)S(1)} %cholesky.272), custom_call_target="Cholesky" | custom-call | tf_op jit(solution)/shard_map/jit(cholesky)/cholesky | solution.py:36
  266.7 9.8 %custom-call.34 = f32[1,128,128]{1,2,0:T(8,128)S(1)} custom-call(f32[1,128,128]{2,1,0:T(8,128)S(1)} %get-tuple-element.26), custom_call_target="InvertDiagBlocksLowerTriangular" | custom-call | tf_op jit(solution)/shard_map/jit(cholesky)/cholesky | solution.py:36
  277.1 11.9 %cholesky.253 = f32[128,128]{1,0:T(8,128)S(1)} custom-call(f32[128,128]{1,0:T(8,128)S(1)} %convolution_subtract_fusion.8), custom_call_target="Cholesky" | custom-call | tf_op jit(solution)/shard_map/jit(cholesky)/cholesky | solution.py:36
  293.4 7.6 %while.1 = (s32[]{:T(128)}, f32[512,512]{1,0:T(8,128)S(1)}, s32[4,2]{0,1:T(2,128)S(1)}, f32[4,128,128]{2,1,0:T(8,128)S(1)}, s32[]{:T(128)}) while((s32[]{:T(128)}, f32[512,512]{1,0:T(8,128)S(1)}, s32[4,2]{0,1:T(2,128)S(1)}, f32[4,128,128]{2,1,0:T(8,128)S(1)}, s32[]{:T(128)}) %tuple.28), condition=%wide.while_cond, body=%wide.while_body.sunk | while | flops 2 | bytes 131189 | solution.py:38
  294.1 1.3 bitcast_dynamic-update-slice_fusion.2
  296.0 1.3 bitcast_dynamic-update-slice_fusion.2
  297.9 1.3 bitcast_dynamic-update-slice_fusion.2
  299.8 1.3 bitcast_dynamic-update-slice_fusion.2
  301.1 39.3 %custom-call.35 = f32[4,128,128]{1,2,0:T(8,128)S(1)} custom-call(f32[4,128,128]{2,1,0:T(8,128)S(1)} %get-tuple-element.12), custom_call_target="InvertDiagBlocksLowerTriangular" | custom-call | tf_op jit(solution)/shard_map/triangular_solve | solution.py:38
  340.4 6.4 %fusion = f32[512,256]{1,0:T(8,128)S(1)} fusion(bf16[512,4096]{1,0:T(8,128)(2,1)} %reshape.73, bf16[256,1,4096]{2,1,0:T(2,128)(2,1)} %all-gather.13.cloned.1.call-done), kind=kOutput, calls=%fused_computation.2 | convolution fusion | flops 1073741824 | bytes 6815744 | tf_op jit(solution)/shard_map/dot_general | solution.py:10
  (55 shorter events, 14.2 us)
Async XLA Ops:
  6.5 32.1 %all-gather.7.cloned.1.call-start = ((), (), s32[]{:S(2)}) async-start(), calls=%async_computation | async-start | bytes 1310720 | tf_op jit(solution)/shard_map/all_gather | solution.py:22
  7.3 65.6 %all-gather.9.cloned.1.call-start = ((), (), s32[]{:S(2)}) async-start(), calls=%async_computation.1 | async-start | bytes 2293760 | tf_op jit(solution)/shard_map/all_gather | solution.py:20
  8.0 188.1 %all-gather.11.cloned.1.call-start = ((), (), s32[]{:S(2)}) async-start(), calls=%async_computation.2 | async-start | bytes 4210688 | tf_op jit(solution)/shard_map/all_gather | solution.py:28
  80.4 260.1 %all-gather.13.cloned.1.call-start = ((), (), s32[]{:S(2)}) async-start(), calls=%async_computation.3 | async-start | bytes 4210688 | tf_op jit(solution)/shard_map/all_gather | solution.py:27
Sparse Core Ops, SparseCore 0:
  9.2 29.3 all-gather.6
  40.4 32.4 all-gather.8
  80.5 115.5 all-gather.10
  199.7 112.8 all-gather.12
where the time goes:
time: 363 us; the launch traced here: 359 us
  other arithmetic  119 us (33%)
  waiting for transfers between devices  100 us (28%)
  blocking collectives  76.6 us (21%)
  matrix products  29.1 us (8%)
  between operations  17.4 us (5%)
  local copies, waits for them, and re-layouts  16.4 us (5%)
    another operation x14, other arithmetic, shards(): factor = jnp.linalg.cholesky(system)  78.7 us
    psum x1, blocking collectives, shards(): trace_value = lax.psum(jnp.sum(wide * wide), ('dp', 'fsdp'))  76.6 us
    another operation x3, other arithmetic, shards(): lax.linalg.triangular_solve(factor, middle, left_side=True, lower=True, t...  39.4 us
    all_gather x1, waiting for transfers between devices, shards(): all_sketch = lax.all_gather(own_sketch, ('dp', 'fsdp'), axis=0, tiled=True)  37.1 us
    all_gather x1, waiting for transfers between devices, shards(): lax.all_gather(out_proj, 'fsdp', axis=1, tiled=True)  30.5 us
    all_gather x1, waiting for transfers between devices, shards(): lax.all_gather(in_proj, 'fsdp', axis=1, tiled=True)  30.4 us
    dot_general x4, matrix products, project(): lax.dot_general(rows, matrix, (((1,), (1,)), ((), ())), preferred_element...  22 us
    unnamed x2, local copies, waits for them, and re-layouts  8.33 us
  transfers between devices with their start and end apart: 4, of which 3 were waited for; matrix products, arithmetic and copies ran while one was open for 41% of the time, Pallas kernels for 0%

commit v1 on v0

--- a/solution.py
+++ b/solution.py
@@ -1,9 +1,131 @@
+import functools
 import jax
 import jax.numpy as jnp
 from jax import lax
+from jax.experimental import pallas as pl
+from jax.experimental.pallas import tpu as pltpu
 from jax.sharding import PartitionSpec as P
 
 LEN = 128
+
+f32, bf16 = jnp.float32, jnp.bfloat16
+
+
+def dot(a, b, precision=None):
+    return lax.dot_general(
+        a, b, (((1,), (0,)), ((), ())), preferred_element_type=f32, precision=precision
+    )
+
+
+def split(value):
+    high = value.astype(bf16)
+    return high, (value - high.astype(f32)).astype(bf16)
+
+
+def solve_kernel(rows_of, rank, gram_ref, cross_ref, out_ref, product, inverse, sys_high, sys_low, answer):
+    n = gram_ref.shape[0]
+    gram = gram_ref[...]
+    row = lax.broadcasted_iota(jnp.int32, (n, n), 0)
+    col = lax.broadcasted_iota(jnp.int32, (n, n), 1)
+    diagonal = row == col
+    trace = jnp.sum(jnp.where(diagonal, gram, 0.0))
+    damping = 0.1 * trace / n
+    top = damping + jnp.minimum(trace, jnp.max(jnp.sum(jnp.abs(gram), axis=0)))
+    system = gram + jnp.where(diagonal, damping, 0.0)
+    scale = 2.0 / (damping + top)
+    bound0 = (top - damping) / (top + damping)
+    high, low = split(system)
+    sys_high[...] = high
+    sys_low[...] = low
+    first, second = rows_of()
+    shape = (8, n)
+    want_row = lax.broadcasted_iota(jnp.int32, shape, 0)
+    want_col = lax.broadcasted_iota(jnp.int32, shape, 1)
+    unit = jnp.where(
+        ((want_row == 0) & (want_col == first)) | ((want_row == 1) & (want_col == second)), 1.0, 0.0
+    )
+
+    def invert(multiply):
+        def gain_of(bound):
+            return 2.0 / (2.0 - bound * bound)
+
+        def step(bound):
+            gain = gain_of(bound)
+            y = product[...]
+            x = inverse[...]
+            inverse[...] = gain * (2.0 * x - multiply(x, y))
+            product[...] = gain * (2.0 * y - multiply(y, y))
+            return bound * bound * 0.5 * gain
+
+        gain = gain_of(bound0)
+        y = scale * system
+        inverse[...] = (gain * scale) * (jnp.where(diagonal, 2.0, 0.0) - y)
+        product[...] = gain * (2.0 * y - multiply(y, y))
+        lax.while_loop(lambda b: b > 0.06, step, bound0 * bound0 * 0.5 * gain)
+
+    def apply(z, high, low):
+        parts = jnp.concatenate(split(z), axis=0)
+        whole = dot(parts, high) + dot(parts, low)
+        return whole[:8] + whole[8:]
+
+    def refine(correct, residual):
+        def step(carry):
+            z, left, _, count = carry
+            z = z + correct(left)
+            left = unit - residual(z)
+            return z, left, jnp.max(jnp.abs(left)), count + 1
+
+        def go_on(carry):
+            return (carry[2] > 2e-5) & (carry[3] < 8)
+
+        z, _, error, _ = lax.while_loop(
+            go_on, step, (jnp.zeros(shape, f32), unit, jnp.float32(1.0), jnp.int32(0))
+        )
+        answer[...] = z
+        return error
+
+    def quick():
+        invert(lambda a, b: dot(a.astype(bf16), b.astype(bf16)))
+        near = inverse[...].astype(bf16)
+
+        def correct(left):
+            parts = jnp.concatenate(split(left), axis=0)
+            moved = dot(parts, near)
+            return moved[:8] + moved[8:]
+
+        return refine(correct, lambda z: apply(z, sys_high[...], sys_low[...]))
+
+    def careful():
+        exact = lax.Precision.HIGHEST
+        invert(lambda a, b: dot(a, b, exact))
+        refine(
+            lambda left: dot(left, inverse[...], exact),
+            lambda z: dot(z, gram_ref[...], exact) + damping * z,
+        )
+
+    error = lax.cond(top < 500.0 * damping, quick, lambda: jnp.float32(1.0))
+    pl.when(jnp.logical_not(error <= 2e-5))(careful)
+    cross_high, cross_low = split(cross_ref[...])
+    out_ref[...] = (damping / rank) * apply(answer[...], cross_high, cross_low)
+
+
+def solve(gram, cross, rows_of, rank):
+    n, nq = cross.shape
+    return pl.pallas_call(
+        functools.partial(solve_kernel, rows_of, rank),
+        out_shape=jax.ShapeDtypeStruct((8, nq), f32),
+        in_specs=[pl.BlockSpec(memory_space=pltpu.VMEM)] * 2,
+        out_specs=pl.BlockSpec(memory_space=pltpu.VMEM),
+        scratch_shapes=[
+            pltpu.VMEM((n, n), f32),
+            pltpu.VMEM((n, n), f32),
+            pltpu.VMEM((n, n), bf16),
+            pltpu.VMEM((n, n), bf16),
+            pltpu.VMEM((8, n), f32),
+        ],
+        compiler_params=pltpu.CompilerParams(vmem_limit_bytes=40 * 2**20),
+        cost_estimate=pl.CostEstimate(flops=2 * 10 * n**3, bytes_accessed=4 * n * (n + nq), transcendentals=0),
+    )(gram, cross)
 
 
 def project(rows, matrix):
@@ -28,19 +150,12 @@
     all_sketch = lax.all_gather(own_sketch, ("dp", "fsdp"), axis=0, tiled=True)
     gram = project(all_sketch, all_sketch)
     cross = project(all_sketch, all_queries)
-    examples = gram.shape[0]
-    wide = own_sketch.astype(jnp.float32)
-    trace_value = lax.psum(jnp.sum(wide * wide), ("dp", "fsdp"))
-    damping = 0.1 * trace_value / examples
-    system = gram + damping * jnp.eye(examples, dtype=jnp.float32)
-    factor = jnp.linalg.cholesky(system)
-    middle = lax.linalg.triangular_solve(factor, cross, left_side=True, lower=True)
-    solved = lax.linalg.triangular_solve(
-        factor, middle, left_side=True, lower=True, transpose_a=True
-    )
-    first = lax.axis_index(("dp", "fsdp")) * seq_count
-    own_rows = lax.dynamic_slice_in_dim(solved, first, seq_count, 0)
-    return damping / sketch_rank * own_rows.T
+
+    def rows_of():
+        first = lax.axis_index(("dp", "fsdp")) * seq_count
+        return first, first + 1
+
+    return solve(gram, cross, rows_of, sketch_rank)[:seq_count].T
 
 
 def solution(mesh):

time: 363 us -> 332 us (0.915); the launches traced: 359 us -> 332 us
  waiting for transfers between devices: 100 us -> 281 us
  other arithmetic: 119 us -> 0 us
  blocking collectives: 76.6 us -> 0 us
  local copies, waits for them, and re-layouts: 16.4 us -> 8.5 us
  Pallas kernels: 0 us -> 7.25 us
  matrix products: 29.1 us -> 22.1 us
  between operations: 17.4 us -> 13.1 us
    another operation x17 -> x0, other arithmetic: 118 us -> none  [the longest x14 78.7 us: shards(): factor = jnp.linalg.cholesky(system)]
    all_gather x1, waiting for transfers between devices: 0.02 us -> 103 us  [shards(): all_queries = lax.all_gather(queries, ('dp', 'fsdp'), axis=0, tiled=True)]
    all_gather x1, waiting for transfers between devices: 37.1 us -> 115 us  [shards(): all_sketch = lax.all_gather(own_sketch, ('dp', 'fsdp'), axis=0, tiled=True)]
    psum x1 -> x0, blocking collectives: 76.6 us -> none  [shards(): trace_value = lax.psum(jnp.sum(wide * wide), ('dp', 'fsdp'))]
    another operation x17 -> x0, local copies, waits for them, and re-layouts: 7.7 us -> none
    pallas_call x0 -> x1, Pallas kernels: none -> 7.25 us  [solve(): pl.pallas_call(functools.partial(solve_kernel, rows_of, rank), out_shape=...]
    another operation x20 -> x0, matrix products: 6.29 us -> none  [the longest x7 2.25 us: shards(): lax.linalg.triangular_solve(factor, middle, left_side=True, lower=True, t...]
  transfers between devices with their start and end apart: 4 -> 4, of which waited for: 3 -> 4; matrix products, arithmetic and copies ran while one was open for 41% -> 5% of each run, Pallas kernels for 0% -> 0%
where the time goes in v1:
time: 332 us
  waiting for transfers between devices  281 us (85%)
  matrix products  22.1 us (7%)
  between operations  13.1 us (4%)
  local copies, waits for them, and re-layouts  8.5 us (3%)
  Pallas kernels  7.25 us (2%)
    all_gather x1, waiting for transfers between devices, shards(): all_sketch = lax.all_gather(own_sketch, ('dp', 'fsdp'), axis=0, tiled=True)  115 us
    all_gather x1, waiting for transfers between devices, shards(): all_queries = lax.all_gather(queries, ('dp', 'fsdp'), axis=0, tiled=True)  103 us
    all_gather x1, waiting for transfers between devices, shards(): lax.all_gather(out_proj, 'fsdp', axis=1, tiled=True)  30.5 us
    all_gather x1, waiting for transfers between devices, shards(): lax.all_gather(in_proj, 'fsdp', axis=1, tiled=True)  30.4 us
    dot_general x4, matrix products, project(): lax.dot_general(rows, matrix, (((1,), (1,)), ((), ())), preferred_element...  22 us
    unnamed x2, local copies, waits for them, and re-layouts  7.91 us
    pallas_call x1, Pallas kernels, solve(): pl.pallas_call(functools.partial(solve_kernel, rows_of, rank), out_shape=...  7.25 us
  transfers between devices with their start and end apart: 4, of which 4 were waited for; matrix products, arithmetic and copies ran while one was open for 5% of the time, Pallas kernels for 0%

profile of v1, /device:TPU:1, one launch (start us, length us, event | category | flops | bytes accessed | tf_op | source)
XLA Modules:
  0.0 332.2 jit_solution(14909920789971642347)
XLA Ops:
  6.5 0.0 all-gather.7.cloned.1.call-start
  6.5 0.7 all-gather.7.cloned.1.call-update
  7.3 0.0 all-gather.9.cloned.1.call-start
  7.3 0.7 all-gather.9.cloned.1.call-update
  8.0 0.0 all-gather.11.cloned.1.call-start
  8.1 30.5 %all-gather.7.cloned.1.call-done = bf16[64,8192]{1,0:T(8,128)(2,1)} async-done(((bf16[64,2048]{1,0:T(8,128)(2,1)}), bf16[64,8192]{1,0:T(8,128)(2,1)}) %all-gather.7.cloned.1.call-update) | async-done | bytes 1048592 | tf_op jit(solution)/shard_map/all_gather | solution.py:144
  38.6 3.9 %convolution_bitcast_fusion.1 = bf16[8,2,8,128]{3,2,1,0:T(8,128)(2,1)S(1)} fusion(bf16[256,8192]{1,0:T(8,128)(2,1)} %param.6, bf16[64,8192]{1,0:T(8,128)(2,1)} %all-gather.7.cloned.1.call-done), kind=kOutput, calls=%fused_computation.5 | convolution fusion | flops 268435456 | bytes 5275648 | tf_op jit(solution)/shard_map/dot_general | solution.py:132
  42.5 30.4 %all-gather.9.cloned.1.call-done = bf16[64,14336]{1,0:T(8,128)(2,1)} async-done(((bf16[64,3584]{1,0:T(8,128)(2,1)}), bf16[64,14336]{1,0:T(8,128)(2,1)}) %all-gather.9.cloned.1.call-update) | async-done | bytes 1835024 | tf_op jit(solution)/shard_map/all_gather | solution.py:142
  72.9 5.9 %convolution_bitcast_fusion = bf16[8,2,8,128]{3,2,1,0:T(8,128)(2,1)S(1)} fusion(bf16[256,14336]{1,0:T(8,128)(2,1)} %param.5, bf16[64,14336]{1,0:T(8,128)(2,1)} %all-gather.9.cloned.1.call-done), kind=kOutput, calls=%fused_computation.4 | convolution fusion | flops 469762048 | bytes 9207808 | tf_op jit(solution)/shard_map/dot_general | solution.py:132
  78.8 0.1 fusion.3
  79.0 0.7 reshape.10
  79.7 0.0 all-gather.11.cloned.1.call-update
  79.7 0.0 all-gather.13.cloned.1.call-start
  79.8 0.5 all-gather.13.cloned.1.call-update
  80.3 115.2 %all-gather.11.cloned.1.call-done = bf16[256,2,4096]{2,1,0:T(2,128)(2,1)} async-done(((bf16[1,2,4096]{2,1,0:T(2,128)(2,1)}), bf16[256,2,4096]{2,1,0:T(2,128)(2,1)}) %all-gather.11.cloned.1.call-update) | async-done | bytes 4194320 | tf_op jit(solution)/shard_map/all_gather | solution.py:150
  195.5 7.2 %reshape.11 = bf16[512,4096]{1,0:T(8,128)(2,1)} reshape(bf16[256,2,4096]{2,1,0:T(2,128)(2,1)} %all-gather.11.cloned.1.call-done) | data formatting | bytes 8388608
  202.7 5.8 %fusion.8.gram_ref = f32[512,512]{1,0:T(8,128)S(1)} fusion(bf16[512,4096]{1,0:T(8,128)(2,1)} %reshape.11), kind=kOutput, calls=%fused_computation.12 | convolution fusion | flops 2147483648 | bytes 5242880 | tf_op jit(solution)/shard_map/dot_general | solution.py:132
  208.5 103.0 %all-gather.13.cloned.1.call-done = bf16[256,1,4096]{2,1,0:T(2,128)(2,1)} async-done(((bf16[1,1,4096]{2,1,0:T(2,128)(2,1)}), bf16[256,1,4096]{2,1,0:T(2,128)(2,1)}) %all-gather.13.cloned.1.call-update) | async-done | bytes 2097168 | tf_op jit(solution)/shard_map/all_gather | solution.py:149
  311.5 6.4 %fusion.cross_ref = f32[512,256]{1,0:T(8,128)S(1)} fusion(bf16[512,4096]{1,0:T(8,128)(2,1)} %reshape.11, bf16[256,1,4096]{2,1,0:T(2,128)(2,1)} %all-gather.13.cloned.1.call-done), kind=kOutput, calls=%fused_computation | convolution fusion | flops 1073741824 | bytes 6815744 | tf_op jit(solution)/shard_map/dot_general | solution.py:132
  317.9 7.2 %shard_map.55 = f32[8,256]{1,0:T(8,128)S(1)} custom-call(f32[512,512]{1,0:T(8,128)S(1)} %fusion.8.gram_ref, f32[512,256]{1,0:T(8,128)S(1)} %fusion.cross_ref), custom_call_target="tpu_custom_call" | custom-call | flops 2684354560 | bytes 1572864 | tf_op jit(solution)/shard_map/pallas_call | solution.py:114
  325.1 0.6 slice_bitcast_fusion
Async XLA Ops:
  6.5 32.1 %all-gather.7.cloned.1.call-start = ((), (), s32[]{:S(2)}) async-start(), calls=%async_computation | async-start | bytes 1310720 | tf_op jit(solution)/shard_map/all_gather | solution.py:144
  7.3 65.6 %all-gather.9.cloned.1.call-start = ((), (), s32[]{:S(2)}) async-start(), calls=%async_computation.1 | async-start | bytes 2293760 | tf_op jit(solution)/shard_map/all_gather | solution.py:142
  8.0 187.5 %all-gather.11.cloned.1.call-start = ((), (), s32[]{:S(2)}) async-start(), calls=%async_computation.2 | async-start | bytes 4210688 | tf_op jit(solution)/shard_map/all_gather | solution.py:150
  79.7 231.8 %all-gather.13.cloned.1.call-start = ((), (), s32[]{:S(2)}) async-start(), calls=%async_computation.3 | async-start | bytes 4210688 | tf_op jit(solution)/shard_map/all_gather | solution.py:149
Sparse Core Ops, SparseCore 0:
  9.2 29.3 all-gather.6
  40.4 32.4 all-gather.8
  79.8 115.5 all-gather.10
  199.0 112.3 all-gather.12

commit v2 on v1

--- a/solution.py
+++ b/solution.py
@@ -1,4 +1,5 @@
 import functools
+import math
 import jax
 import jax.numpy as jnp
 from jax import lax
@@ -7,8 +8,383 @@
 from jax.sharding import PartitionSpec as P
 
 LEN = 128
-
+RINGS = (4, 4, 8)
+MESH = pl.DeviceIdType.MESH
 f32, bf16 = jnp.float32, jnp.bfloat16
+
+
+def dot_rows(a, b, precision=None):
+    return lax.dot_general(
+        a, b, (((1,), (1,)), ((), ())), preferred_element_type=f32, precision=precision
+    )
+
+
+def place():
+    dp = lax.axis_index("dp")
+    return lax.axis_index("fsdp"), lax.rem(lax.div(dp, 2), 4), lax.div(dp, 8), lax.rem(dp, 2)
+
+
+def gather_kernel(
+    hidden, grads, w_in, w_out, query,
+    gram_out, cross_out,
+    hid, grd, win, wout, sketch_all, query_all, gram_own, gram_other, cross_own, cross_other,
+    side, first_sent, first_got, spread, q_flat, q_sent, q_pair, q_x, q_y,
+    send, got, first_sem, local,
+):
+    nx, ny, nz = RINGS
+    x, y, z, c = place()
+    other = 1 - c
+
+    def at(dx=0, dy=0, dz=0, dc=0):
+        px, py = lax.rem(x + (dx + nx), nx), lax.rem(y + (dy + ny), ny)
+        pz, pc = lax.rem(z + (dz + nz), nz), lax.rem(c + dc, 2)
+        return ((pz * ny + py) * 2 + pc, px)
+
+    x_at = [x, lax.rem(x + 3, 4), lax.rem(x + 1, 4), lax.rem(x + 2, 4)]
+    y_at = [y, lax.rem(y + 3, 4), lax.rem(y + 1, 4), lax.rem(y + 2, 4)]
+    z_at = {k: lax.rem(z + k + nz, nz) for k in range(-4, 5)}
+
+    partners = (
+        [(k, 0, 0, 0) for k in (1, 2, 3)]
+        + [(0, k, 0, 0) for k in (1, 2, 3)]
+        + [(0, 0, k, j) for k in range(nz) for j in range(2) if k + j > 0]
+    )
+    barrier = pltpu.get_barrier_semaphore()
+    for partner in partners:
+        pl.semaphore_signal(barrier, inc=1, device_id=at(*partner), device_id_type=MESH)
+
+    in_width, out_width = w_in.shape[1], w_out.shape[1]
+    loads = []
+
+    def load(src, dst):
+        copy = pltpu.make_async_copy(src, dst, local.at[len(loads)])
+        copy.start()
+        loads.append(copy)
+        return copy
+
+    own_in = load(w_in, win.at[0])
+    own_out = load(w_out, wout.at[0])
+    hid_loads, grd_loads = [], []
+    for k in range(4):
+        hid_loads.append(load(hidden.at[:, pl.ds(pl.multiple_of(x_at[k] * in_width, 128), in_width)], hid.at[k]))
+        grd_loads.append(load(grads.at[:, pl.ds(pl.multiple_of(x_at[k] * out_width, 128), out_width)], grd.at[k]))
+
+    sent = []
+    count = [0]
+
+    def message(src, dst, device, landing):
+        number = count[0]
+        count[0] += 1
+        copy = pltpu.make_async_remote_copy(
+            src_ref=src, dst_ref=dst, send_sem=send.at[number], recv_sem=got.at[number],
+            device_id=device, device_id_type=MESH,
+        )
+        copy.start()
+        sent.append(copy)
+        return pltpu.make_async_remote_copy(
+            src_ref=landing, dst_ref=landing, send_sem=send.at[number], recv_sem=got.at[number],
+            device_id=device, device_id_type=MESH,
+        )
+
+    for b in range(32):
+        q_flat[pl.ds(b, 1), :] = query[:, 128 * b : 128 * (b + 1)].astype(f32)
+    for h in range(2):
+        q_sent[h] = q_flat[pl.ds(16 * h, 16), :].astype(bf16)
+
+    pl.semaphore_wait(barrier, len(partners))
+
+    color = lax.rem(y, 2)
+    mine, theirs = pl.ds(pl.multiple_of(32 * c, 32), 32), pl.ds(pl.multiple_of(32 * other, 32), 32)
+
+    class Matrix:
+        def __init__(self, source, slots, width):
+            self.source, self.slots, self.half, self.quarter = source, slots, width // 2, width // 4
+
+        def columns(self, which, part=None):
+            begin = which * self.half
+            if part is None:
+                return pl.ds(pl.multiple_of(begin, 128), self.half)
+            return pl.ds(pl.multiple_of(begin + part * self.quarter, 128), self.quarter)
+
+        def slot(self, k, rows, columns):
+            return self.slots.at[k, rows, columns]
+
+    matrices = [Matrix(w_in, win, in_width), Matrix(w_out, wout, out_width)]
+    hop = []
+    for m in matrices:
+        columns = m.columns(color)
+        source = m.source.at[mine, columns]
+        hop.append((
+            message(source, m.slot(1, mine, columns), at(dx=1), m.slot(1, mine, columns)),
+            message(source, m.slot(2, mine, columns), at(dx=-1), m.slot(2, mine, columns)),
+        ))
+    q_a = message(q_sent.at[other], q_pair.at[c], at(dc=1), q_pair.at[other])
+    q_pair[c] = q_sent[c]
+
+    q_a.wait_recv()
+    q_x[:, x] = q_pair[...]
+    q_b = [
+        message(q_pair, q_x.at[:, x], at(dx=k), q_x.at[:, lax.rem(x + nx - k, nx)]) for k in (1, 2, 3)
+    ]
+
+    own_in.wait()
+    hid_loads[0].wait()
+    in_side = dot_rows(hid[0], win[0])
+    own_out.wait()
+    grd_loads[0].wait()
+    out_side = dot_rows(wout[0], grd[0])
+
+    for copy in q_b:
+        copy.wait_recv()
+    q_y[y] = q_x[...]
+    q_c = [
+        message(q_x, q_y.at[y], at(dy=k), q_y.at[lax.rem(y + ny - k, ny)]) for k in (1, 2, 3)
+    ]
+
+    near = []
+    sib = {1: [], 2: [], 3: []}
+    last = []
+
+    def to_sibling(m, k, columns):
+        sib[k].append(
+            message(m.slot(k, mine, columns), m.slot(k, mine, columns), at(dc=1), m.slot(k, theirs, columns))
+        )
+
+    def to_y(m, k, part):
+        step = 1 if part == 0 else -1
+        ours, foreign = m.columns(color, part), m.columns(1 - color, part)
+        near.append((
+            m, k, foreign,
+            message(m.slot(k, mine, ours), m.slot(k, mine, ours), at(dy=step), m.slot(k, mine, foreign)),
+        ))
+
+    for m, (from_left, from_right) in zip(matrices, hop):
+        part0, part1 = m.columns(color, 0), m.columns(color, 1)
+        from_left.wait_recv()
+        last.append((m, 0, message(m.slot(1, mine, part0), m.slot(3, mine, part0), at(dx=1), m.slot(3, mine, part0))))
+        to_y(m, 1, 0)
+        to_y(m, 1, 1)
+        to_sibling(m, 1, m.columns(color))
+        from_right.wait_recv()
+        last.append((m, 1, message(m.slot(2, mine, part1), m.slot(3, mine, part1), at(dx=-1), m.slot(3, mine, part1))))
+        to_y(m, 2, 0)
+        to_y(m, 2, 1)
+        to_sibling(m, 2, m.columns(color))
+
+    for copy in q_c:
+        copy.wait_recv()
+    spread[...] = q_y[...].reshape(ny * 2 * nx * 16, 128).astype(f32)
+    q_rows = ny * 2 * nx
+
+    def q_block(k):
+        return query_all.at[pl.ds(pl.multiple_of(z_at[k] * q_rows, q_rows), q_rows), :]
+
+    def q_half(k, h):
+        return query_all.at[pl.ds(pl.multiple_of(z_at[k] * q_rows + h * (q_rows // 2), q_rows // 2), q_rows // 2), :]
+
+    for b in range(16):
+        query_all[pl.ds(pl.multiple_of(z * q_rows, q_rows), q_rows), 128 * b : 128 * (b + 1)] = spread[
+            pl.ds(b, q_rows, stride=16), :
+        ].astype(bf16)
+
+    def q_step(t):
+        if t < 4:
+            return (
+                message(q_block(1 - t), q_block(1 - t), at(dz=1), q_block(-t)),
+                message(q_block(t - 1), q_block(t - 1), at(dz=-1), q_block(t)),
+            )
+        return (
+            message(q_half(-3, 0), q_half(-3, 0), at(dz=1), q_half(-4, 0)),
+            message(q_half(3, 1), q_half(3, 1), at(dz=-1), q_half(4, 1)),
+        )
+
+    def arrive(pair):
+        for copy in pair:
+            copy.wait_recv()
+
+    q_ring = q_step(1)
+
+    for m, part, copy in last:
+        copy.wait_recv()
+        to_y(m, 3, part)
+        to_sibling(m, 3, m.columns(color, part))
+    arrive(q_ring)
+    q_ring = q_step(2)
+    for k in (1, 2, 3):
+        for m, at_k, columns, copy in near:
+            if at_k == k:
+                copy.wait_recv()
+                to_sibling(m, k, columns)
+    for k in (1, 2, 3):
+        hid_loads[k].wait()
+        grd_loads[k].wait()
+        for copy in sib[k]:
+            copy.wait_recv()
+        in_side += dot_rows(hid[k], win[k])
+        out_side += dot_rows(wout[k], grd[k])
+        if k == 1:
+            arrive(q_ring)
+            q_ring = q_step(3)
+    arrive(q_ring)
+    q_ring = q_step(4)
+
+    exact = lax.Precision.HIGHEST
+    rank = in_side.shape[1]
+    for s in range(2):
+        outer = lax.dot_general(
+            out_side[:, LEN * s : LEN * (s + 1)], in_side[LEN * s : LEN * (s + 1), :],
+            (((1,), (0,)), ((), ())), preferred_element_type=f32, precision=exact,
+        )
+        side[...] = outer / math.sqrt(LEN)
+        rows = jnp.concatenate(
+            [side[pl.ds(0, rank // 2, stride=2), :], side[pl.ds(1, rank // 2, stride=2), :]], axis=1
+        ).astype(bf16)
+        for h in range(2):
+            first_sent[h, 16 * s : 16 * (s + 1), :] = rows[16 * h : 16 * (h + 1), :]
+
+    slot = z * 2 + c
+    first = []
+    for dz in range(nz):
+        for dc in range(2):
+            if dz + dc > 0:
+                copy = pltpu.make_async_remote_copy(
+                    src_ref=first_sent.at[lax.rem(c + dc, 2)], dst_ref=first_got.at[slot],
+                    send_sem=send.at[count[0]], recv_sem=first_sem, device_id=at(dz=dz, dc=dc), device_id_type=MESH,
+                )
+                count[0] += 1
+                copy.start()
+                sent.append(copy)
+    first_got[slot] = first_sent[c]
+    everyone = first_got.at[pl.ds(0, 2 * nz - 1)]
+    pltpu.make_async_remote_copy(
+        src_ref=everyone, dst_ref=everyone, send_sem=send.at[0], recv_sem=first_sem,
+        device_id=at(dc=1), device_id_type=MESH,
+    ).wait_recv()
+    spread[...] = first_got[...].reshape(2 * nz * 32, 128).astype(f32)
+    rows = 2 * 2 * nz
+
+    def block(kx, ky):
+        return sketch_all.at[pl.ds(pl.multiple_of((kx * ny + ky) * rows, rows), rows), :]
+
+    def half(kx, ky, h):
+        return sketch_all.at[pl.ds(pl.multiple_of((kx * ny + ky) * rows + h * (rows // 2), rows // 2), rows // 2), :]
+
+    for s in range(2):
+        for b in range(16):
+            begin = pl.multiple_of((x * ny + y) * rows + s * 16, 16)
+            sketch_all[pl.ds(begin, 16), 128 * b : 128 * (b + 1)] = spread[
+                pl.ds(s * 16 + b, 16, stride=32), :
+            ].astype(bf16)
+
+    def pick(on_first, on_second):
+        return on_first + c * (on_second - on_first)
+
+    u_at = [pick(a, b) for a, b in zip(y_at, x_at)]
+    v_at = [pick(a, b) for a, b in zip(x_at, y_at)]
+
+    def cell(u, v):
+        return pick(v_at[v], u_at[u]), pick(u_at[u], v_at[v])
+
+    def along_u(step):
+        return at(dx=c * step, dy=other * step)
+
+    def along_v(step):
+        return at(dx=other * step, dy=c * step)
+
+    u_left = message(block(*cell(0, 0)), block(*cell(0, 0)), along_u(1), block(*cell(1, 0)))
+    u_right = message(block(*cell(0, 0)), block(*cell(0, 0)), along_u(-1), block(*cell(2, 0)))
+
+    def send_v(u):
+        here = block(*cell(u, 0))
+        return (
+            message(here, here, along_v(1), block(*cell(u, 1))),
+            message(here, here, along_v(-1), block(*cell(u, 2))),
+        )
+
+    def forward_v(u, pair):
+        pair[0].wait_recv()
+        a = half(*cell(u, 1), 0)
+        left = message(a, a, along_v(1), half(*cell(u, 3), 0))
+        pair[1].wait_recv()
+        b = half(*cell(u, 2), 1)
+        right = message(b, b, along_v(-1), half(*cell(u, 3), 1))
+        return left, right
+
+    v_pairs = {0: send_v(0)}
+    u_left.wait_recv()
+    a = half(*cell(1, 0), 0)
+    u_far = [message(a, a, along_u(1), half(*cell(3, 0), 0))]
+    v_pairs[1] = send_v(1)
+    u_right.wait_recv()
+    b = half(*cell(2, 0), 1)
+    u_far.append(message(b, b, along_u(-1), half(*cell(3, 0), 1)))
+    v_pairs[2] = send_v(2)
+    tails = [forward_v(0, v_pairs[0])]
+    arrive(u_far)
+    v_pairs[3] = send_v(3)
+    arrive(q_ring)
+    for u in (1, 2, 3):
+        tails.append(forward_v(u, v_pairs[u]))
+    for pair in tails:
+        arrive(pair)
+
+    gram_own[...] = dot_rows(sketch_all[...], sketch_all[...])
+    gram_sum = message(gram_own, gram_other, at(dc=1), gram_other)
+    cross_own[...] = dot_rows(sketch_all[...], query_all[...])
+    cross_sum = message(cross_own, cross_other, at(dc=1), cross_other)
+    gram_sum.wait_recv()
+    gram_out[...] = gram_own[...] + gram_other[...]
+    cross_sum.wait_recv()
+    cross_out[...] = cross_own[...] + cross_other[...]
+
+    for copy in sent:
+        copy.wait_send()
+
+
+def gather(hidden, grads, w_in, w_out, query):
+    examples, queries, half = 512, 256, 2048
+    rank = w_in.shape[0]
+    anywhere = pl.BlockSpec(memory_space=pl.ANY)
+    vmem = pl.BlockSpec(memory_space=pltpu.VMEM)
+    rows = hidden.shape[0]
+    return pl.pallas_call(
+        gather_kernel,
+        out_shape=(
+            jax.ShapeDtypeStruct((examples, examples), f32),
+            jax.ShapeDtypeStruct((examples, queries), f32),
+        ),
+        in_specs=[anywhere] * 4 + [vmem],
+        out_specs=(vmem, vmem),
+        scratch_shapes=[
+            pltpu.VMEM((4, rows, w_in.shape[1]), bf16),
+            pltpu.VMEM((4, rows, w_out.shape[1]), bf16),
+            pltpu.VMEM((4, rank, w_in.shape[1]), bf16),
+            pltpu.VMEM((4, rank, w_out.shape[1]), bf16),
+            pltpu.VMEM((examples, half), bf16),
+            pltpu.VMEM((queries, half), bf16),
+            pltpu.VMEM((examples, examples), f32),
+            pltpu.VMEM((examples, examples), f32),
+            pltpu.VMEM((examples, queries), f32),
+            pltpu.VMEM((examples, queries), f32),
+            pltpu.VMEM((rank, rank), f32),
+            pltpu.VMEM((2, 32, 128), bf16),
+            pltpu.VMEM((16, 32, 128), bf16),
+            pltpu.VMEM((512, 128), f32),
+            pltpu.VMEM((32, 128), f32),
+            pltpu.VMEM((2, 16, 128), bf16),
+            pltpu.VMEM((2, 16, 128), bf16),
+            pltpu.VMEM((2, 4, 16, 128), bf16),
+            pltpu.VMEM((4, 2, 4, 16, 128), bf16),
+            pltpu.SemaphoreType.DMA((128,)),
+            pltpu.SemaphoreType.DMA((128,)),
+            pltpu.SemaphoreType.DMA,
+            pltpu.SemaphoreType.DMA((10,)),
+        ],
+        compiler_params=pltpu.CompilerParams(
+            collective_id=0, has_side_effects=True, vmem_limit_bytes=48 * 2**20
+        ),
+        cost_estimate=pl.CostEstimate(flops=4 * 10**9, bytes_accessed=14 * 10**6, transcendentals=0),
+    )(hidden, grads, w_in, w_out, query)
 
 
 def dot(a, b, precision=None):
@@ -128,34 +504,15 @@
     )(gram, cross)
 
 
-def project(rows, matrix):
-    return lax.dot_general(
-        rows, matrix, (((1,), (1,)), ((), ())), preferred_element_type=jnp.float32
-    )
-
-
-def shards(hidden, out_grads, in_proj, out_proj, queries):
-    row_count = hidden.shape[0]
-    sketch_rank = in_proj.shape[0]
-    seq_count = row_count // LEN
-    columns = hidden
-    in_side = project(columns, lax.all_gather(in_proj, "fsdp", axis=1, tiled=True))
-    columns = out_grads
-    out_side = project(columns, lax.all_gather(out_proj, "fsdp", axis=1, tiled=True))
-    in_blocks = in_side.reshape(seq_count, LEN, sketch_rank)
-    out_blocks = out_side.reshape(seq_count, LEN, sketch_rank)
-    outer = jnp.einsum("slb,sla->sba", out_blocks, in_blocks) / jnp.sqrt(jnp.float32(LEN))
-    own_sketch = outer.reshape(seq_count, sketch_rank * sketch_rank).astype(jnp.bfloat16)
-    all_queries = lax.all_gather(queries, ("dp", "fsdp"), axis=0, tiled=True)
-    all_sketch = lax.all_gather(own_sketch, ("dp", "fsdp"), axis=0, tiled=True)
-    gram = project(all_sketch, all_sketch)
-    cross = project(all_sketch, all_queries)
+def shards(hidden, grads, w_in, w_out, query):
+    gram, cross = gather(hidden, grads, w_in, w_out, query)
 
     def rows_of():
-        first = lax.axis_index(("dp", "fsdp")) * seq_count
-        return first, first + 1
-
-    return solve(gram, cross, rows_of, sketch_rank)[:seq_count].T
+        x, y, z, c = place()
+        first = (x * RINGS[1] + y) * 32 + z * 2 + c
+        return first, first + 16
+
+    return solve(gram, cross, rows_of, w_in.shape[0])[:2].T
 
 
 def solution(mesh):

time: 332 us -> 78.7 us (0.24)
  waiting for transfers between devices: 281 us -> 0 us
  Pallas kernels: 7.25 us -> 75.3 us
  matrix products: 22.1 us -> 0 us
  between operations: 13.1 us -> 0.01 us
  local copies, waits for them, and re-layouts: 8.5 us -> 3.27 us
    all_gather x4 -> x0, waiting for transfers between devices: 279 us -> none  [the longest x1 115 us: shards(): all_sketch = lax.all_gather(own_sketch, ('dp', 'fsdp'), axis=0, tiled=True)]
    pallas_call x0 -> x1, Pallas kernels: none -> 68.5 us  [gather(): pl.pallas_call(gather_kernel, out_shape=(jax.ShapeDtypeStruct((examples,...]
    dot_general x5 -> x0, matrix products: 22.1 us -> none  [the longest x4 22 us: project(): lax.dot_general(rows, matrix, (((1,), (1,)), ((), ())), preferred_element...]
    unnamed x2 -> x6, local copies, waits for them, and re-layouts: 7.91 us -> 2.68 us
  transfers between devices with their start and end apart: 4 -> 0, of which waited for: 4 -> 0; matrix products, arithmetic and copies ran while one was open for 5% -> 0% of each run, Pallas kernels for 0% -> 0%
where the time goes in v2:
time: 78.7 us; the launch traced here: 78.5 us
  Pallas kernels  75.3 us (96%)
  local copies, waits for them, and re-layouts  3.27 us (4%)
    pallas_call x1, Pallas kernels, gather(): pl.pallas_call(gather_kernel, out_shape=(jax.ShapeDtypeStruct((examples,...  68.5 us
    pallas_call x1, Pallas kernels, solve(): pl.pallas_call(functools.partial(solve_kernel, rows_of, rank), out_shape=...  6.71 us
    unnamed x6, local copies, waits for them, and re-layouts  2.68 us

profile of v2, /device:TPU:1, one launch (start us, length us, event | category | flops | bytes accessed | tf_op | source)
XLA Modules:
  0.0 78.5 jit_solution(3991126593611463069)
XLA Ops:
  0.0 0.0 copy-start
  0.0 1.0 %copy-done = bf16[64,3584]{1,0:T(8,128)(2,1)S(1)} copy-done((bf16[64,3584]{1,0:T(8,128)(2,1)S(1)}, bf16[64,3584]{1,0:T(8,128)(2,1)}, u32[]{:S(2)}) %copy-start) | copy-done | bytes 458776
  1.0 0.0 copy-start.1
  1.0 0.9 %copy-done.1 = bf16[64,2048]{1,0:T(8,128)(2,1)S(1)} copy-done((bf16[64,2048]{1,0:T(8,128)(2,1)S(1)}, bf16[64,2048]{1,0:T(8,128)(2,1)}, u32[]{:S(2)}) %copy-start.1) | copy-done | bytes 262168
  2.0 0.0 copy-start.2
  2.0 0.7 copy-done.2
  2.7 68.5 %shard_map.55 = (f32[512,512]{1,0:T(8,128)S(1)}, f32[512,256]{1,0:T(8,128)S(1)}) custom-call(bf16[256,14336]{1,0:T(8,128)(2,1)} %hidden.1, bf16[256,8192]{1,0:T(8,128)(2,1)} %grads.1, bf16[64,3584]{1,0:T(8,128)(2,1)S(1)} %copy-done, bf16[64,2048]{1,0:T(8,128)(2,1)S(1)} %copy-done.1, bf16[1,4096]{1,0:T(2,128)(2,1)S(1)} %copy-done.2), custom_call_target="tpu_custom_call" | custom-call | flops 4000000000 | bytes 14000000 | tf_op jit(solution)/shard_map/pallas_call | solution.py:350
  71.2 6.7 %shard_map.56 = f32[8,256]{1,0:T(8,128)S(1)} custom-call(f32[512,512]{1,0:T(8,128)S(1)} %get-tuple-element.7.gram_ref, f32[512,256]{1,0:T(8,128)S(1)} %get-tuple-element.8.cross_ref), custom_call_target="tpu_custom_call" | custom-call | flops 2684354560 | bytes 1572864 | tf_op jit(solution)/shard_map/pallas_call | solution.py:490
  77.9 0.6 slice_bitcast_fusion
Async XLA Ops:
  0.0 1.0 %copy-start = (bf16[64,3584]{1,0:T(8,128)(2,1)S(1)}, bf16[64,3584]{1,0:T(8,128)(2,1)}, u32[]{:S(2)}) copy-start(bf16[64,3584]{1,0:T(8,128)(2,1)} %w_in.1) | copy-start | bytes 1376260
  1.0 0.9 %copy-start.1 = (bf16[64,2048]{1,0:T(8,128)(2,1)S(1)}, bf16[64,2048]{1,0:T(8,128)(2,1)}, u32[]{:S(2)}) copy-start(bf16[64,2048]{1,0:T(8,128)(2,1)} %w_out.1) | copy-start | bytes 786436
  2.0 0.7 copy-start.2

commit v3 on v2

v3 whole, which is shorter than its diff:
```python
import functools
import math
import jax
import jax.numpy as jnp
from jax import lax
from jax.experimental import pallas as pl
from jax.experimental.pallas import tpu as pltpu
from jax.sharding import PartitionSpec as P

LEN = 128
RINGS = (4, 4, 8)
LIMIT = 48 * 2**20
MESH = pl.DeviceIdType.MESH
f32, bf16 = jnp.float32, jnp.bfloat16


def dot_rows(a, b, precision=None):
    return lax.dot_general(
        a, b, (((1,), (1,)), ((), ())), preferred_element_type=f32, precision=precision
    )


def place():
    dp = lax.axis_index("dp")
    return lax.axis_index("fsdp"), lax.rem(lax.div(dp, 2), 4), lax.div(dp, 8), lax.rem(dp, 2)


def gather_kernel(
    hidden, grads, w_in, w_out, query,
    gram_out, cross_out,
    hid, grd, w_raw_in, w_raw_out, query_raw, weights, total,
    sketch_all, sketch_cols, query_all, query_cols, gram_pair, cross_pair,
    side, first_sent, first_got, spread, q_flat, q_sent, q_pair, q_x, q_y,
    send, got, first_sem, local,
):
    nx, ny, nz = RINGS
    x, y, z, c = place()
    other = 1 - c

    def at(dx=0, dy=0, dz=0, dc=0):
        px, py = lax.rem(x + (dx + nx), nx), lax.rem(y + (dy + ny), ny)
        pz, pc = lax.rem(z + (dz + nz), nz), lax.rem(c + dc, 2)
        return ((pz * ny + py) * 2 + pc, px)

    x_at = [x, lax.rem(x + 3, 4), lax.rem(x + 1, 4), lax.rem(x + 2, 4)]
    y_at = [y, lax.rem(y + 3, 4), lax.rem(y + 1, 4), lax.rem(y + 2, 4)]
    z_at = {k: lax.rem(z + k + nz, nz) for k in range(-4, 5)}

    partners = (
        [(k, 0, 0, 0) for k in (1, 2, 3)]
        + [(0, k, 0, 0) for k in (1, 2, 3)]
        + [(0, 0, k, j) for k in range(nz) for j in range(2) if k + j > 0]
    )
    barrier = pltpu.get_barrier_semaphore()
    for partner in partners:
        pl.semaphore_signal(barrier, inc=1, device_id=at(*partner), device_id_type=MESH)

    in_width, out_width = w_in.shape[1], w_out.shape[1]
    loads = []

    def load(src, dst):
        copy = pltpu.make_async_copy(src, dst, local.at[len(loads)])
        copy.start()
        loads.append(copy)
        return copy

    own_in = load(w_in, w_raw_in)
    own_out = load(w_out, w_raw_out)
    own_query = load(query, query_raw)
    sent = []
    count = [0]

    def message(src, dst, device, landing):
        number = count[0]
        count[0] += 1
        copy = pltpu.make_async_remote_copy(
            src_ref=src, dst_ref=dst, send_sem=send.at[number], recv_sem=got.at[number],
            device_id=device, device_id_type=MESH,
        )
        copy.start()
        sent.append(copy)
        return pltpu.make_async_remote_copy(
            src_ref=landing, dst_ref=landing, send_sem=send.at[number], recv_sem=got.at[number],
            device_id=device, device_id_type=MESH,
        )

    in_half, out_half = in_width // 2, out_width // 2
    own_in.wait()
    own_out.wait()
    hid_loads, grd_loads = [], []
    for k in range(4):
        hid_loads.append(load(hidden.at[:, pl.ds(pl.multiple_of(x_at[k] * in_width, 128), in_width)], hid.at[k]))
        grd_loads.append(load(grads.at[:, pl.ds(pl.multiple_of(x_at[k] * out_width, 128), out_width)], grd.at[k]))
    for raw, half, base in ((w_raw_in, in_half, 0), (w_raw_out, out_half, in_half)):
        for b in range(half // 128):
            pair = jnp.concatenate(
                [raw[:, 128 * b : 128 * (b + 1)], raw[:, half + 128 * b : half + 128 * (b + 1)]], axis=0
            )
            weights[0, base + 128 * b : base + 128 * (b + 1), :] = pair.T

    pl.semaphore_wait(barrier, len(partners))

    color = lax.rem(y, 2)
    per_core = (in_half + out_half) // 2
    starts, sizes = (0, 64, 192, 400), (64, 128, 208, 304)
    onward = {1: (0, 3), 2: (1, 2)}

    def piece(slot, core, which, part):
        begin = core * per_core + which * (per_core // 2) + starts[part]
        return weights.at[slot, pl.ds(pl.multiple_of(begin, 16), sizes[part]), :]

    def hop(slot, part):
        return message(
            piece(0, c, color, part), piece(slot, c, color, part), at(dx=1 if slot == 1 else -1),
            piece(slot, c, color, part),
        )

    order = [(slot, part) for part in range(4) for slot in (1, 2)]
    hops = {key: hop(*key) for key in order}

    own_query.wait()
    for b in range(32):
        q_flat[pl.ds(b, 1), :] = query_raw[:, 128 * b : 128 * (b + 1)].astype(f32)
    for h in range(2):
        q_sent[h] = q_flat[pl.ds(16 * h, 16), :].astype(bf16)
    q_a = message(q_sent.at[other], q_pair.at[c], at(dc=1), q_pair.at[other])
    q_pair[c] = q_sent[c]

    def product(k):
        values = (
            jnp.dot(hid[k, :, :in_half], weights[k, :in_half, :], preferred_element_type=f32),
            jnp.dot(hid[k, :, in_half:], weights[k, :in_half, :], preferred_element_type=f32),
            jnp.dot(grd[k, :, :out_half], weights[k, in_half:, :], preferred_element_type=f32),
            jnp.dot(grd[k, :, out_half:], weights[k, in_half:, :], preferred_element_type=f32),
        )
        for i, value in enumerate(values):
            total[i] = value if k == 0 else total[i] + value

    hid_loads[0].wait()
    grd_loads[0].wait()
    product(0)

    siblings = {1: [], 2: [], 3: []}
    crossing = {1: [], 2: [], 3: []}

    def to_sibling(slot, which, part):
        siblings[slot].append(
            message(piece(slot, c, which, part), piece(slot, c, which, part), at(dc=1), piece(slot, other, which, part))
        )

    def spread_out(slot, part):
        crossing[slot].append((part, message(
            piece(slot, c, color, part), piece(slot, c, color, part), at(dy=1 if part in onward[1] else -1),
            piece(slot, c, 1 - color, part),
        )))
        to_sibling(slot, color, part)

    far = []
    for slot, part in order:
        hops[slot, part].wait_recv()
        if part in onward[slot]:
            far.append((part, message(
                piece(slot, c, color, part), piece(3, c, color, part), at(dx=1 if slot == 1 else -1),
                piece(3, c, color, part),
            )))
        spread_out(slot, part)
        if (slot, part) == (2, 0):
            q_a.wait_recv()
            q_x[:, x] = q_pair[...]
            q_b = [
                message(q_pair, q_x.at[:, x], at(dx=k), q_x.at[:, lax.rem(x + nx - k, nx)]) for k in (1, 2, 3)
            ]

    def crossed(slot):
        for part, copy in crossing[slot]:
            copy.wait_recv()
            to_sibling(slot, 1 - color, part)

    for copy in q_b:
        copy.wait_recv()
    q_y[y] = q_x[...]
    q_c = [
        message(q_x, q_y.at[y], at(dy=k), q_y.at[lax.rem(y + ny - k, ny)]) for k in (1, 2, 3)
    ]
    for part, copy in far:
        copy.wait_recv()
        spread_out(3, part)
    crossed(1)
    crossed(2)
    def arrive(pair):
        for copy in pair:
            copy.wait_recv()

    q_rows = ny * 2 * nx

    def q_block(k):
        return query_all.at[pl.ds(pl.multiple_of(z_at[k] * q_rows, q_rows), q_rows), :]

    def q_half(k, h):
        return query_all.at[pl.ds(pl.multiple_of(z_at[k] * q_rows + h * (q_rows // 2), q_rows // 2), q_rows // 2), :]

    def q_step(t):
        if t < 4:
            return (
                message(q_block(1 - t), q_block(1 - t), at(dz=1), q_block(-t)),
                message(q_block(t - 1), q_block(t - 1), at(dz=-1), q_block(t)),
            )
        return (
            message(q_half(-3, 0), q_half(-3, 0), at(dz=1), q_half(-4, 0)),
            message(q_half(3, 1), q_half(3, 1), at(dz=-1), q_half(4, 1)),
        )

    def finish(slot):
        hid_loads[slot].wait()
        grd_loads[slot].wait()
        arrive(siblings[slot])
        product(slot)

    for copy in q_c:
        copy.wait_recv()
    spread[...] = q_y[...].reshape(ny * 2 * nx * 16, 128).astype(f32)
    for b in range(16):
        query_all[pl.ds(pl.multiple_of(z * q_rows, q_rows), q_rows), 128 * b : 128 * (b + 1)] = spread[
            pl.ds(b, q_rows, stride=16), :
        ].astype(bf16)

    q_ring = q_step(1)
    finish(1)
    crossed(3)
    finish(2)
    finish(3)
    arrive(q_ring)
    q_ring = q_step(2)

    rank = w_in.shape[0]
    in_side = total[0][:, :rank] + total[1][:, rank:]
    out_side = (total[2][:, :rank] + total[3][:, rank:]).T
    for s in range(2):
        tokens = slice(LEN * s, LEN * (s + 1))
        out_high, out_low = split(out_side[:, tokens])
        in_high, in_low = split(in_side[tokens, :])
        outer = jnp.dot(
            jnp.concatenate([out_high, out_high, out_low], axis=1),
            jnp.concatenate([in_high, in_low, in_high], axis=0), preferred_element_type=f32,
        )
        side[...] = outer / math.sqrt(LEN)
        rows = jnp.concatenate(
            [side[pl.ds(0, rank // 2, stride=2), :], side[pl.ds(1, rank // 2, stride=2), :]], axis=1
        ).astype(bf16)
        for h in range(2):
            first_sent[h, 16 * s : 16 * (s + 1), :] = rows[16 * h : 16 * (h + 1), :]

    slot = z * 2 + c
    first = []
    for dz in range(nz):
        for dc in range(2):
            if dz + dc > 0:
                copy = pltpu.make_async_remote_copy(
                    src_ref=first_sent.at[lax.rem(c + dc, 2)], dst_ref=first_got.at[slot],
                    send_sem=send.at[count[0]], recv_sem=first_sem, device_id=at(dz=dz, dc=dc), device_id_type=MESH,
                )
                count[0] += 1
                copy.start()
                sent.append(copy)
    first_got[slot] = first_sent[c]
    everyone = first_got.at[pl.ds(0, 2 * nz - 1)]
    pltpu.make_async_remote_copy(
        src_ref=everyone, dst_ref=everyone, send_sem=send.at[0], recv_sem=first_sem,
        device_id=at(dc=1), device_id_type=MESH,
    ).wait_recv()
    spread[...] = first_got[...].reshape(2 * nz * 32, 128).astype(f32)
    rows = 2 * 2 * nz

    def pick(on_first, on_second):
        return on_first + c * (on_second - on_first)

    u_at = [pick(a, b) for a, b in zip(y_at, x_at)]
    v_at = [pick(a, b) for a, b in zip(x_at, y_at)]

    def block(u, v):
        return sketch_all.at[pl.ds(pl.multiple_of((v_at[v] * nx + u_at[u]) * rows, rows), rows), :]

    def half(u, v, h):
        begin = (v_at[v] * nx + u_at[u]) * rows + h * (rows // 2)
        return sketch_all.at[pl.ds(pl.multiple_of(begin, rows // 2), rows // 2), :]

    def along_u(step):
        return at(dx=c * step, dy=other * step)

    def along_v(step):
        return at(dx=other * step, dy=c * step)

    for s in range(2):
        for b in range(16):
            begin = pl.multiple_of((v_at[0] * nx + u_at[0]) * rows + s * 16, 16)
            sketch_all[pl.ds(begin, 16), 128 * b : 128 * (b + 1)] = spread[
                pl.ds(s * 16 + b, 16, stride=32), :
            ].astype(bf16)

    u_left = message(block(0, 0), block(0, 0), along_u(1), block(1, 0))
    u_right = message(block(0, 0), block(0, 0), along_u(-1), block(2, 0))

    def send_v(u):
        return (
            message(block(u, 0), block(u, 0), along_v(1), block(u, 1)),
            message(block(u, 0), block(u, 0), along_v(-1), block(u, 2)),
        )

    def forward_v(u, pair):
        pair[0].wait_recv()
        left = message(half(u, 1, 0), half(u, 1, 0), along_v(1), half(u, 3, 0))
        pair[1].wait_recv()
        right = message(half(u, 2, 1), half(u, 2, 1), along_v(-1), half(u, 3, 1))
        return left, right

    slab = rows * nx
    gram_sums = []
    cross_sums = []

    def slab_at(v):
        return pl.ds(pl.multiple_of(v_at[v] * slab, slab), slab)

    def share(kind, pair, *index):
        kind.append(message(pair.at[(c,) + index], pair.at[(c,) + index], at(dc=1), pair.at[(other,) + index]))

    def multiply(v):
        here = slab_at(v)
        for b in range(16):
            lanes = slice(128 * b, 128 * (b + 1))
            sketch_cols[lanes, here] = sketch_all[here, lanes].T
        mine = sketch_all[here, :]
        if v < 3:
            for w in range(v + 1):
                there = slab_at(w)
                part = jnp.dot(mine, sketch_cols[:, there], preferred_element_type=f32)
                gram_pair[c, here, there] = part
                share(gram_sums, gram_pair, here, there)
                if w < v:
                    gram_pair[c, there, here] = part.T
                    share(gram_sums, gram_pair, there, here)
        else:
            gram_pair[c, here, :] = jnp.dot(mine, sketch_cols[...], preferred_element_type=f32)
            share(gram_sums, gram_pair, here, slice(None))
            for w in range(v):
                there = slab_at(w)
                gram_pair[c, there, here] = gram_pair[c, here, there].T
                share(gram_sums, gram_pair, there, here)

    def multiply_queries(v):
        here = slab_at(v)
        mine = sketch_all[here, :]
        cross_pair[c, here, :] = jnp.dot(mine, query_cols[...], preferred_element_type=f32)
        share(cross_sums, cross_pair, here, slice(None))

    u_far = message(block(0, 0), block(0, 0), along_u(2), block(3, 0))
    v_pairs = {0: send_v(0)}
    arrive(q_ring)
    q_ring = q_step(3)
    u_left.wait_recv()
    v_pairs[1] = send_v(1)
    u_right.wait_recv()
    v_pairs[2] = send_v(2)
    u_far.wait_recv()
    v_pairs[3] = send_v(3)
    multiply(0)
    tails = [forward_v(0, v_pairs[0])]
    arrive(q_ring)
    q_ring = q_step(4)
    for u in (1, 2, 3):
        tails.append(forward_v(u, v_pairs[u]))
    multiply(1)
    multiply(2)
    arrive(q_ring)
    for b in range(16):
        lanes = slice(128 * b, 128 * (b + 1))
        query_cols[lanes, :] = query_all[:, lanes].T
    for v in range(3):
        multiply_queries(v)
    for pair in tails:
        arrive(pair)
    multiply(3)
    multiply_queries(3)

    lane = lax.broadcasted_iota(jnp.int32, (rows, 128), 1)
    for copy in gram_sums:
        copy.wait_recv()
    for kx in range(nx):
        for ky in range(ny):
            source = slice((ky * nx + kx) * rows, (ky * nx + kx + 1) * rows)
            target = slice((kx * ny + ky) * rows, (kx * ny + ky + 1) * rows)
            tiles = [gram_pair[1, source, 128 * j : 128 * (j + 1)] for j in range(4)]
            for i in range(4):
                turned = tiles[i]
                for j in range(4):
                    if j != i:
                        moved = pltpu.roll(tiles[j], (32 * (j - i)) % 128, 1)
                        turned = jnp.where((lane >= 32 * j) & (lane < 32 * (j + 1)), moved, turned)
                lanes = slice(128 * i, 128 * (i + 1))
                gram_out[target, lanes] = gram_pair[0, target, lanes] + turned
    for copy in cross_sums:
        copy.wait_recv()
    for kx in range(nx):
        for ky in range(ny):
            source = slice((ky * nx + kx) * rows, (ky * nx + kx + 1) * rows)
            target = slice((kx * ny + ky) * rows, (kx * ny + ky + 1) * rows)
            cross_out[target, :] = cross_pair[0, target, :] + cross_pair[1, source, :]

    for copy in sent:
        copy.wait_send()


def gather(hidden, grads, w_in, w_out, query):
    examples, queries, half = 512, 256, 2048
    rank = w_in.shape[0]
    anywhere = pl.BlockSpec(memory_space=pltpu.HBM)
    vmem = pl.BlockSpec(memory_space=pltpu.VMEM)
    rows = hidden.shape[0]
    return pl.pallas_call(
        gather_kernel,
        out_shape=(
            jax.ShapeDtypeStruct((examples, examples), f32),
            jax.ShapeDtypeStruct((examples, queries), f32),
        ),
        in_specs=[anywhere] * 5,
        out_specs=(vmem, vmem),
        scratch_shapes=[
            pltpu.VMEM((4, rows, w_in.shape[1]), bf16),
            pltpu.VMEM((4, rows, w_out.shape[1]), bf16),
            pltpu.VMEM(w_in.shape, bf16),
            pltpu.VMEM(w_out.shape, bf16),
            pltpu.VMEM(query.shape, bf16),
            pltpu.VMEM((4, (w_in.shape[1] + w_out.shape[1]) // 2, 2 * rank), bf16),
            pltpu.VMEM((4, rows, 2 * rank), f32),
            pltpu.VMEM((examples, half), bf16),
            pltpu.VMEM((half, examples), bf16),
            pltpu.VMEM((queries, half), bf16),
            pltpu.VMEM((half, queries), bf16),
            pltpu.VMEM((2, examples, examples), f32),
            pltpu.VMEM((2, examples, queries), f32),
            pltpu.VMEM((rank, rank), f32),
            pltpu.VMEM((2, 32, 128), bf16),
            pltpu.VMEM((16, 32, 128), bf16),
            pltpu.VMEM((512, 128), f32),
            pltpu.VMEM((32, 128), f32),
            pltpu.VMEM((2, 16, 128), bf16),
            pltpu.VMEM((2, 16, 128), bf16),
            pltpu.VMEM((2, 4, 16, 128), bf16),
            pltpu.VMEM((4, 2, 4, 16, 128), bf16),
            pltpu.SemaphoreType.DMA((128,)),
            pltpu.SemaphoreType.DMA((128,)),
            pltpu.SemaphoreType.DMA,
            pltpu.SemaphoreType.DMA((11,)),
        ],
        compiler_params=pltpu.CompilerParams(
            collective_id=0, has_side_effects=True, vmem_limit_bytes=LIMIT
        ),
        cost_estimate=pl.CostEstimate(flops=4 * 10**9, bytes_accessed=14 * 10**6, transcendentals=0),
    )(hidden, grads, w_in, w_out, query)


def dot(a, b, precision=None):
    return lax.dot_general(
        a, b, (((1,), (0,)), ((), ())), preferred_element_type=f32, precision=precision
    )


def split(value):
    high = value.astype(bf16)
    return high, (value - high.astype(f32)).astype(bf16)


def solve_kernel(rows_of, rank, gram_ref, cross_ref, out_ref, product, inverse, sys_high, sys_low, answer):
    n = gram_ref.shape[0]
    gram = gram_ref[...]
    row = lax.broadcasted_iota(jnp.int32, (n, n), 0)
    col = lax.broadcasted_iota(jnp.int32, (n, n), 1)
    diagonal = row == col
    trace = jnp.sum(jnp.where(diagonal, gram, 0.0))
    damping = 0.1 * trace / n
    top = damping + jnp.minimum(trace, jnp.max(jnp.sum(jnp.abs(gram), axis=0)))
    system = gram + jnp.where(diagonal, damping, 0.0)
    scale = 2.0 / (damping + top)
    bound0 = (top - damping) / (top + damping)
    high, low = split(system)
    sys_high[...] = high
    sys_low[...] = low
    first, second = rows_of()
    shape = (8, n)
    want_row = lax.broadcasted_iota(jnp.int32, shape, 0)
    want_col = lax.broadcasted_iota(jnp.int32, shape, 1)
    unit = jnp.where(
        ((want_row == 0) & (want_col == first)) | ((want_row == 1) & (want_col == second)), 1.0, 0.0
    )

    def invert(multiply):
        def gain_of(bound):
            return 2.0 / (2.0 - bound * bound)

        def step(bound):
            gain = gain_of(bound)
            y = product[...]
            x = inverse[...]
            inverse[...] = gain * (2.0 * x - multiply(x, y))
            product[...] = gain * (2.0 * y - multiply(y, y))
            return bound * bound * 0.5 * gain

        gain = gain_of(bound0)
        y = scale * system
        inverse[...] = (gain * scale) * (jnp.where(diagonal, 2.0, 0.0) - y)
        product[...] = gain * (2.0 * y - multiply(y, y))
        lax.while_loop(lambda b: b > 0.06, step, bound0 * bound0 * 0.5 * gain)

    def apply(z, high, low):
        parts = jnp.concatenate(split(z), axis=0)
        whole = dot(parts, high) + dot(parts, low)
        return whole[:8] + whole[8:]

    def refine(correct, residual):
        def step(carry):
            z, left, _, count = carry
            z = z + correct(left)
            left = unit - residual(z)
            return z, left, jnp.max(jnp.abs(left)), count + 1

        def go_on(carry):
            return (carry[2] > 2e-5) & (carry[3] < 8)

        z, _, error, _ = lax.while_loop(
            go_on, step, (jnp.zeros(shape, f32), unit, jnp.float32(1.0), jnp.int32(0))
        )
        answer[...] = z
        return error

    def quick():
        invert(lambda a, b: dot(a.astype(bf16), b.astype(bf16)))
        near = inverse[...].astype(bf16)

        def correct(left):
            parts = jnp.concatenate(split(left), axis=0)
            moved = dot(parts, near)
            return moved[:8] + moved[8:]

        return refine(correct, lambda z: apply(z, sys_high[...], sys_low[...]))

    def careful():
        exact = lax.Precision.HIGHEST
        invert(lambda a, b: dot(a, b, exact))
        refine(
            lambda left: dot(left, inverse[...], exact),
            lambda z: dot(z, gram_ref[...], exact) + damping * z,
        )

    error = lax.cond(top < 500.0 * damping, quick, lambda: jnp.float32(1.0))
    pl.when(jnp.logical_not(error <= 2e-5))(careful)
    cross_high, cross_low = split(cross_ref[...])
    out_ref[...] = ((damping / rank) * apply(answer[...], cross_high, cross_low))[:2]


def solve(gram, cross, rows_of, rank):
    n, nq = cross.shape
    return pl.pallas_call(
        functools.partial(solve_kernel, rows_of, rank),
        out_shape=jax.ShapeDtypeStruct((2, nq), f32),
        in_specs=[pl.BlockSpec(memory_space=pltpu.VMEM)] * 2,
        out_specs=pl.BlockSpec(memory_space=pltpu.VMEM),
        scratch_shapes=[
            pltpu.VMEM((n, n), f32),
            pltpu.VMEM((n, n), f32),
            pltpu.VMEM((n, n), bf16),
            pltpu.VMEM((n, n), bf16),
            pltpu.VMEM((8, n), f32),
        ],
        compiler_params=pltpu.CompilerParams(vmem_limit_bytes=40 * 2**20),
        cost_estimate=pl.CostEstimate(flops=2 * 10 * n**3, bytes_accessed=4 * n * (n + nq), transcendentals=0),
    )(gram, cross)


def shards(hidden, grads, w_in, w_out, query):
    operands = (hidden, grads, w_in, w_out, query)
    gram, cross = gather(*(pltpu.with_memory_space_constraint(v, pltpu.HBM) for v in operands))

    def rows_of():
        x, y, z, c = place()
        first = (x * RINGS[1] + y) * 32 + z * 2 + c
        return first, first + 16

    return solve(gram, cross, rows_of, w_in.shape[0]).T


def solution(mesh):
    in_specs = (
        P(("dp", "fsdp"), None),
        P(("dp", "fsdp"), None),
        P(None, "fsdp"),
        P(None, "fsdp"),
        P(("dp", "fsdp"), None),
    )
    out_specs = P(None, ("dp", "fsdp"))
    return jax.shard_map(shards, mesh=mesh, in_specs=in_specs, out_specs=out_specs, check_vma=False)
```

time: 78.7 us -> 64.6 us (0.82)
  Pallas kernels: 75.3 us -> 64.5 us
  local copies, waits for them, and re-layouts: 3.27 us -> 0 us
    pallas_call x1, Pallas kernels: 68.5 us -> 57.2 us  [gather(): pl.pallas_call(gather_kernel, out_shape=(jax.ShapeDtypeStruct((examples,...]
    unnamed x6 -> x0, local copies, waits for them, and re-layouts: 2.68 us -> none
where the time goes in v3:
time: 64.6 us; the launch traced here: 64.5 us
  Pallas kernels  64.5 us (100%)
    pallas_call x1, Pallas kernels, gather(): pl.pallas_call(gather_kernel, out_shape=(jax.ShapeDtypeStruct((examples,...  57.2 us
    pallas_call x1, Pallas kernels, solve(): pl.pallas_call(functools.partial(solve_kernel, rows_of, rank), out_shape=...  7.26 us

profile of v3, /device:TPU:1, one launch (start us, length us, event | category | flops | bytes accessed | tf_op | source)
XLA Modules:
  0.0 64.5 jit_solution(11393250283685847313)
XLA Ops:
  0.0 57.2 %shard_map.55 = (f32[512,512]{1,0:T(8,128)S(1)}, f32[512,256]{1,0:T(8,128)S(1)}) custom-call(bf16[256,14336]{1,0:T(8,128)(2,1)} %hidden.1, bf16[256,8192]{1,0:T(8,128)(2,1)} %grads.1, bf16[64,3584]{1,0:T(8,128)(2,1)} %w_in.1, bf16[64,2048]{1,0:T(8,128)(2,1)} %w_out.1, bf16[1,4096]{1,0:T(2,128)(2,1)} %query.1), custom_call_target="tpu_custom_call" | custom-call | flops 4000000000 | bytes 14000000 | tf_op jit(solution)/shard_map/pallas_call | solution.py:418
  57.3 7.3 %shard_map.56 = f32[2,256]{1,0:T(2,128)} custom-call(f32[512,512]{1,0:T(8,128)S(1)} %get-tuple-element.7.gram_ref, f32[512,256]{1,0:T(8,128)S(1)} %get-tuple-element.8.cross_ref), custom_call_target="tpu_custom_call" | custom-call | flops 2684354560 | bytes 1572864 | tf_op jit(solution)/shard_map/pallas_call | solution.py:561

commit v4 on v3

--- a/solution.py
+++ b/solution.py
@@ -102,7 +102,7 @@
 
     color = lax.rem(y, 2)
     per_core = (in_half + out_half) // 2
-    starts, sizes = (0, 64, 192, 400), (64, 128, 208, 304)
+    starts, sizes = (0, 176, 352, 528), (176, 176, 176, 176)
     onward = {1: (0, 3), 2: (1, 2)}
 
     def piece(slot, core, which, part):

time: 64.6 us -> 63.4 us (0.981)
  Pallas kernels: 64.5 us -> 63.4 us
    pallas_call x1, Pallas kernels: 57.2 us -> 56.1 us  [gather(): pl.pallas_call(gather_kernel, out_shape=(jax.ShapeDtypeStruct((examples,...]
where the time goes in v4:
time: 63.4 us
  Pallas kernels  63.4 us (100%)
    pallas_call x1, Pallas kernels, gather(): pl.pallas_call(gather_kernel, out_shape=(jax.ShapeDtypeStruct((examples,...  56.1 us
    pallas_call x1, Pallas kernels, solve(): pl.pallas_call(functools.partial(solve_kernel, rows_of, rank), out_shape=...  7.26 us

profile of v4, /device:TPU:1, one launch (start us, length us, event | category | flops | bytes accessed | tf_op | source)
XLA Modules:
  0.0 63.4 jit_solution(10298214449899052796)
XLA Ops:
  0.0 56.1 %shard_map.55 = (f32[512,512]{1,0:T(8,128)S(1)}, f32[512,256]{1,0:T(8,128)S(1)}) custom-call(bf16[256,14336]{1,0:T(8,128)(2,1)} %hidden.1, bf16[256,8192]{1,0:T(8,128)(2,1)} %grads.1, bf16[64,3584]{1,0:T(8,128)(2,1)} %w_in.1, bf16[64,2048]{1,0:T(8,128)(2,1)} %w_out.1, bf16[1,4096]{1,0:T(2,128)(2,1)} %query.1), custom_call_target="tpu_custom_call" | custom-call | flops 4000000000 | bytes 14000000 | tf_op jit(solution)/shard_map/pallas_call | solution.py:418
  56.1 7.3 %shard_map.56 = f32[2,256]{1,0:T(2,128)} custom-call(f32[512,512]{1,0:T(8,128)S(1)} %get-tuple-element.7.gram_ref, f32[512,256]{1,0:T(8,128)S(1)} %get-tuple-element.8.cross_ref), custom_call_target="tpu_custom_call" | custom-call | flops 2684354560 | bytes 1572864 | tf_op jit(solution)/shard_map/pallas_call | solution.py:561
